TPU v7x, 512 devices: a whole 4x4x16 slice. The times are simulated.
512 devices in a mesh: cube: 16 (over z), row: 4 (over y_lo, core), col: 8 (over y_hi, x).
Axes of the slice: x: 4, y: 4 (y_hi: 2, y_lo: 2; y = y_hi * 2 + y_lo), z: 16, core: 2. Of those that a mesh axis runs over, the one named last changes fastest.
Arguments:
- front: bfloat16 [16, 3072, 2048], P('cube', 'row', 'col'), may hold values from -6 to 6
- panel_inverse: bfloat16 [16, 1024, 256], P('cube'), may hold values from -0.16 to 0.16
- contrib: bfloat16 [16, 192, 256, 256], P('cube', ('row', 'col')), may hold values from -4 to 4
- pattern: int32 [16, 192, 2], P('cube', ('row', 'col')), may hold values from -1 to 11, as said below
- front_map: int32 [16, 12], P('cube'), may hold values from 0 to 11, as said below
Outputs:
- factored: bfloat16 [16, 3072, 2048], P('cube', 'row', 'col')
Inputs may be any that keep to these rules, and one draw needn't show every extreme that they name: `pattern`: each slot holds (-1, -1) when empty, else two child block indices. For a live slot of a device with col index q, front_map of its cube maps the column index to a block below 8 with residue q mod 8. Of one device's live slots at most 3 map to front block rows of one residue mod 4; in every cube and col index some residue receives exactly 3 from every device of that col index. `front_map`: for each cube a permutation of the block indices that maps blocks below 8 to blocks below 8 with the same residue mod 8.
All inputs are finite; a program needn't handle non-finite values.
Results may differ from a plain program's by a relative error of at most 0.0055.
Values may be sent and summed in bfloat16 or wider, within the bound.
A program may use at most 64 MiB of HBM per device.

v0:
```python
import jax
import jax.numpy as jnp
from jax import lax
from jax.sharding import PartitionSpec as P

KB = 8
PANELS = 4
CAP = 3


def swapped(block, axis, apart):
    count = lax.axis_size(axis)
    route = []
    for low in range(count):
        high = low | 1 << apart
        if high != low and high < count:
            route += [(low, high), (high, low)]
    return lax.ppermute(block, axis, route)


def spread(block, axis, source):
    block = jnp.where(lax.axis_index(axis) == source, block, jnp.zeros_like(block))
    return lax.psum(block, axis)


def bucket(values, targets, groups):
    is_live = targets[:, 0] >= 0
    destination = jnp.where(is_live, targets[:, 0] % groups, groups)
    onehot = (destination[:, None] == jnp.arange(groups, dtype=jnp.int32)[None, :]).astype(
        jnp.int32
    )
    position = jnp.sum((jnp.cumsum(onehot, axis=0) - 1) * onehot, axis=1)
    buffer = (
        jnp.zeros((groups, CAP) + values.shape[1:], values.dtype)
        .at[destination, position]
        .set(values, mode="drop")
    )
    markers = (
        jnp.full((groups, CAP, 2), -1, jnp.int32)
        .at[destination, position]
        .set(targets, mode="drop")
    )
    return (buffer, markers)


def column_panel(panel, col_id, rows_dev, cols_dev):
    block_size = panel.shape[1]
    upper_rows = KB // rows_dev * block_size
    gathered = lax.all_gather(panel[:upper_rows], "row", axis=0, tiled=True)
    ordered = gathered.reshape(rows_dev, KB // rows_dev, block_size, block_size).transpose(
        1, 0, 2, 3
    )
    ordered = ordered.reshape(KB // cols_dev, cols_dev, block_size, block_size)
    owned_rows = lax.dynamic_index_in_dim(ordered, col_id, 1, keepdims=False)
    return owned_rows.reshape(-1, block_size)


def outer_update(panel, columns):
    return lax.dot_general(
        panel, columns, (((1,), (1,)), ((), ())), preferred_element_type=jnp.float32
    )


def shards(front, panel_inverse, contrib, pattern, front_map):
    rows_dev = lax.axis_size("row")
    cols_dev = lax.axis_size("col")
    row_id = lax.axis_index("row")
    col_id = lax.axis_index("col")
    block_size = contrib.shape[-1]
    slot_pairs = pattern[0]
    is_live = slot_pairs[:, 0] >= 0
    mapping = front_map[0]
    target_rows = jnp.where(is_live, mapping[jnp.maximum(slot_pairs[:, 0], 0)], -1)
    target_cols = jnp.where(is_live, mapping[jnp.maximum(slot_pairs[:, 1], 0)], -1)
    targets = jnp.stack([target_rows, target_cols], axis=1)
    top_bit = lax.axis_size("cube").bit_length() - 2
    arrived, arrived_targets = swapped((contrib[0], targets), "cube", top_bit)
    buffer, markers = bucket(arrived, arrived_targets, rows_dev)
    buffer, markers = (
        lax.all_to_all(buffer, "row", split_axis=0, concat_axis=0, tiled=True),
        lax.all_to_all(markers, "row", split_axis=0, concat_axis=0, tiled=True),
    )
    values = buffer.reshape(-1, block_size, block_size).astype(jnp.float32)
    markers = markers.reshape(-1, 2)
    row_blocks = front.shape[1] // block_size
    col_blocks = front.shape[2] // block_size
    filled = markers[:, 0] >= 0
    row_place = jnp.where(filled, markers[:, 0] // rows_dev, row_blocks)
    col_place = jnp.maximum(markers[:, 1], 0) // cols_dev
    work = front[0].astype(jnp.float32).reshape(row_blocks, block_size, col_blocks, block_size)
    work = work.at[row_place, :, col_place, :].add(values, mode="drop")
    work = work.reshape(row_blocks * block_size, col_blocks * block_size)
    row_ids = jnp.arange(row_blocks * block_size, dtype=jnp.int32) // block_size * rows_dev + row_id
    for step in range(PANELS):
        weight = panel_inverse[0, step * block_size : (step + 1) * block_size]
        product = jnp.dot(work.astype(jnp.bfloat16), weight, preferred_element_type=jnp.float32)
        share_panel = jnp.where((row_ids > step)[:, None], product, jnp.float32(0.0)).astype(
            jnp.bfloat16
        )
        panel = spread(share_panel, "col", step % cols_dev)
        columns = column_panel(panel, col_id, rows_dev, cols_dev)
        work = work - outer_update(panel, columns)
        first = step // cols_dev * block_size
        current = work
        chosen = jnp.where(col_id == step % cols_dev, panel.astype(jnp.float32), current)
        work = work.at[:, first : first + block_size].set(chosen)
    return work.astype(jnp.bfloat16)[None]


def solution(mesh):
    in_specs = (
        P("cube", "row", "col"),
        P("cube", None, None),
        P("cube", ("row", "col"), None, None),
        P("cube", ("row", "col"), None),
        P("cube", None),
    )
    out_specs = P("cube", "row", "col")
    return jax.shard_map(shards, mesh=mesh, in_specs=in_specs, out_specs=out_specs, check_vma=False)
```

profile of v0, /device:TPU:1, one launch (start us, length us, event | category | flops | bytes accessed | tf_op | source)
XLA Modules:
  0.0 672.5 jit_solution(7431471332619933259)
XLA Ops:
  6.5 16.4 %collective-permute-start.1 = (bf16[6,256,256]{2,1,0:T(8,128)(2,1)}, bf16[6,256,256]{2,1,0:T(8,128)(2,1)S(1)}, u32[]{:S(2)}, u32[]{:S(2)}) collective-permute-start(bf16[6,256,256]{2,1,0:T(8,128)(2,1)} %bitcast.96), channel_id=1, source_target_pairs={{0,256},{256,0},{32,288},{288,32},{64,320},{320,64},{96,352},{352,... | collective-permute-start | bytes 2359304 | tf_op jit(solution)/shard_map/ppermute | solution.py:18
  25.7 1.9 collective-permute-start
  27.6 20.7 %collective-permute-done = s32[6,2]{0,1:T(2,128)S(1)} collective-permute-done((s32[6,2]{0,1:T(2,128)S(1)}, s32[6,2]{0,1:T(2,128)S(1)}, u32[]{:S(2)}, u32[]{:S(2)}) %collective-permute-start) | collective-permute-done | bytes 80 | tf_op jit(solution)/shard_map/ppermute | solution.py:18
  48.7 0.8 scatter_fusion
  50.2 5.6 all-to-all-start
  55.8 1.3 broadcast_in_dim.61
  57.1 2.8 scatter_fusion.1
  59.9 3.7 all-to-all-start.1
  63.9 19.0 %all-to-all-done.1 = bf16[4,3,256,256]{3,2,1,0:T(8,128)(2,1)S(1)} async-done(((bf16[4,3,256,256]{3,2,1,0:T(8,128)(2,1)}), bf16[4,3,256,256]{3,2,1,0:T(8,128)(2,1)S(1)}, u32[]{:S(2)}, u32[]{:S(2)}) %all-to-all-start.1) | async-done | bytes 1572896 | tf_op jit(solution)/shard_map/all_to_all | solution.py:80
  82.8 2.1 bitcast_convert_fusion
  84.9 5.7 scatter_fusion.2
  90.6 1.0 fusion.11
  91.7 137.5 %all-reduce.5.cloned.1.call-done = bf16[768,256]{1,0:T(8,128)(2,1)} async-done(((bf16[768,256]{1,0:T(8,128)(2,1)}), bf16[768,256]{1,0:T(8,128)(2,1)}) %all-reduce.5.cloned.1.call-update) | async-done | bytes 393232 | tf_op jit(solution)/shard_map/psum | solution.py:23
  229.3 1.7 slice.121
  231.1 32.9 %all-gather.5.cloned.1.call-done = bf16[2048,256]{1,0:T(8,128)(2,1)} async-done(((bf16[512,256]{1,0:T(8,128)(2,1)}), bf16[2048,256]{1,0:T(8,128)(2,1)}) %all-gather.5.cloned.1.call-update) | async-done | bytes 1048592 | tf_op jit(solution)/shard_map/all_gather | solution.py:49
  264.0 1.3 copy.24
  265.6 1.0 fusion.10
  266.7 96.0 %all-reduce.7.cloned.1.call-done = bf16[768,256]{1,0:T(8,128)(2,1)} async-done(((bf16[768,256]{1,0:T(8,128)(2,1)}), bf16[768,256]{1,0:T(8,128)(2,1)}) %all-reduce.7.cloned.1.call-update) | async-done | bytes 393232 | tf_op jit(solution)/shard_map/psum | solution.py:23
  362.7 1.7 slice.122
  364.6 32.5 %all-gather.7.cloned.1.call-done = bf16[2048,256]{1,0:T(8,128)(2,1)} async-done(((bf16[512,256]{1,0:T(8,128)(2,1)}), bf16[2048,256]{1,0:T(8,128)(2,1)}) %all-gather.7.cloned.1.call-update) | async-done | bytes 1048592 | tf_op jit(solution)/shard_map/all_gather | solution.py:49
  397.1 1.3 copy.25
  398.7 1.0 fusion.9
  399.8 95.6 %all-reduce.9.cloned.1.call-done = bf16[768,256]{1,0:T(8,128)(2,1)} async-done(((bf16[768,256]{1,0:T(8,128)(2,1)}), bf16[768,256]{1,0:T(8,128)(2,1)}) %all-reduce.9.cloned.1.call-update) | async-done | bytes 393232 | tf_op jit(solution)/shard_map/psum | solution.py:23
  495.4 1.7 slice.123
  497.3 32.7 %all-gather.9.cloned.1.call-done = bf16[2048,256]{1,0:T(8,128)(2,1)} async-done(((bf16[512,256]{1,0:T(8,128)(2,1)}), bf16[2048,256]{1,0:T(8,128)(2,1)}) %all-gather.9.cloned.1.call-update) | async-done | bytes 1048592 | tf_op jit(solution)/shard_map/all_gather | solution.py:49
  530.0 1.3 copy.26
  531.6 1.0 fusion.8
  532.7 96.0 %all-reduce.11.cloned.1.call-done = bf16[768,256]{1,0:T(8,128)(2,1)} async-done(((bf16[768,256]{1,0:T(8,128)(2,1)}), bf16[768,256]{1,0:T(8,128)(2,1)}) %all-reduce.11.cloned.1.call-update) | async-done | bytes 393232 | tf_op jit(solution)/shard_map/psum | solution.py:23
  628.8 1.7 slice.124
  630.5 32.7 %all-gather.11.cloned.1.call-done = bf16[2048,256]{1,0:T(8,128)(2,1)} async-done(((bf16[512,256]{1,0:T(8,128)(2,1)}), bf16[2048,256]{1,0:T(8,128)(2,1)}) %all-gather.11.cloned.1.call-update) | async-done | bytes 1048592 | tf_op jit(solution)/shard_map/all_gather | solution.py:49
  663.3 1.3 copy.27
  664.6 1.0 fusion.12
  (58 shorter events, 5.4 us)
Async XLA Ops:
  6.5 17.2 %copy-start = (s32[1,12]{1,0:T(1,128)S(1)}, s32[1,12]{1,0:T(1,128)}, u32[]{:S(2)}) copy-start(s32[1,12]{1,0:T(1,128)} %param.25) | copy-start | bytes 148
  6.5 49.3 %collective-permute-start.1 = (bf16[6,256,256]{2,1,0:T(8,128)(2,1)}, bf16[6,256,256]{2,1,0:T(8,128)(2,1)S(1)}, u32[]{:S(2)}, u32[]{:S(2)}) collective-permute-start(bf16[6,256,256]{2,1,0:T(8,128)(2,1)} %bitcast.96), channel_id=1, source_target_pairs={{0,256},{256,0},{32,288},{288,32},{64,320},{320,64},{96,352},{352,... | collective-permute-start | bytes 2359304 | tf_op jit(solution)/shard_map/ppermute | solution.py:18
  25.7 22.6 %collective-permute-start = (s32[6,2]{0,1:T(2,128)S(1)}, s32[6,2]{0,1:T(2,128)S(1)}, u32[]{:S(2)}, u32[]{:S(2)}) collective-permute-start(s32[6,2]{0,1:T(2,128)S(1)} %pad_add_fusion), channel_id=1, source_target_pairs={{0,256},{256,0},{32,288},{288,32},{64,320},{320,64},{96,352},{352,... | collective-permute-start | bytes 152 | tf_op jit(solution)/shard_map/ppermute | solution.py:18
  50.2 9.7 %all-to-all-start = ((s32[4,3,2]{1,2,0:T(2,128)}), s32[4,3,2]{1,2,0:T(2,128)S(1)}, u32[]{:S(2)}, u32[]{:S(2)}) async-start(s32[4,3,2]{1,2,0:T(2,128)} %copy.22), calls=%async_computation | async-start | bytes 8192 | tf_op jit(solution)/shard_map/all_to_all | solution.py:81
  59.9 3.8 copy-start.5
  59.9 22.9 %all-to-all-start.1 = ((bf16[4,3,256,256]{3,2,1,0:T(8,128)(2,1)}), bf16[4,3,256,256]{3,2,1,0:T(8,128)(2,1)S(1)}, u32[]{:S(2)}, u32[]{:S(2)}) async-start(bf16[4,3,256,256]{3,2,1,0:T(8,128)(2,1)} %scatter_fusion.1), calls=%async_computation.1 | async-start | bytes 3145728 | tf_op jit(solution)/shard_map/all_to_all | solution.py:80
  63.6 165.7 %all-reduce.5.cloned.1.call-start = ((), (), s32[]{:S(2)}) async-start(), calls=%async_computation.2 | async-start | bytes 786432 | tf_op jit(solution)/shard_map/psum | solution.py:23
  84.9 5.8 copy-start.6
  91.7 172.3 %all-gather.5.cloned.1.call-start = ((), (), s32[]{:S(2)}) async-start(), calls=%async_computation.3 | async-start | bytes 1310720 | tf_op jit(solution)/shard_map/all_gather | solution.py:49
  229.3 36.0 %copy-start.2 = (bf16[768,256]{1,0:T(8,128)(2,1)S(1)}, bf16[768,256]{1,0:T(8,128)(2,1)}, u32[]{:S(2)}) copy-start(bf16[768,256]{1,0:T(8,128)(2,1)} %all-reduce.5.cloned.1.call-done) | copy-start | bytes 1179652
  231.0 131.7 %all-reduce.7.cloned.1.call-start = ((), (), s32[]{:S(2)}) async-start(), calls=%async_computation.4 | async-start | bytes 786432 | tf_op jit(solution)/shard_map/psum | solution.py:23
  266.6 130.5 %all-gather.7.cloned.1.call-start = ((), (), s32[]{:S(2)}) async-start(), calls=%async_computation.5 | async-start | bytes 1310720 | tf_op jit(solution)/shard_map/all_gather | solution.py:49
  362.7 35.7 %copy-start.4 = (bf16[768,256]{1,0:T(8,128)(2,1)S(1)}, bf16[768,256]{1,0:T(8,128)(2,1)}, u32[]{:S(2)}) copy-start(bf16[768,256]{1,0:T(8,128)(2,1)} %all-reduce.7.cloned.1.call-done) | copy-start | bytes 1179652
  364.5 130.9 %all-reduce.9.cloned.1.call-start = ((), (), s32[]{:S(2)}) async-start(), calls=%async_computation.6 | async-start | bytes 786432 | tf_op jit(solution)/shard_map/psum | solution.py:23
  399.7 130.3 %all-gather.9.cloned.1.call-start = ((), (), s32[]{:S(2)}) async-start(), calls=%async_computation.7 | async-start | bytes 1310720 | tf_op jit(solution)/shard_map/all_gather | solution.py:49
  495.4 35.9 %copy-start.3 = (bf16[768,256]{1,0:T(8,128)(2,1)S(1)}, bf16[768,256]{1,0:T(8,128)(2,1)}, u32[]{:S(2)}) copy-start(bf16[768,256]{1,0:T(8,128)(2,1)} %all-reduce.9.cloned.1.call-done) | copy-start | bytes 1179652
  497.2 131.6 %all-reduce.11.cloned.1.call-start = ((), (), s32[]{:S(2)}) async-start(), calls=%async_computation.8 | async-start | bytes 786432 | tf_op jit(solution)/shard_map/psum | solution.py:23
  532.7 130.6 %all-gather.11.cloned.1.call-start = ((), (), s32[]{:S(2)}) async-start(), calls=%async_computation.9 | async-start | bytes 1310720 | tf_op jit(solution)/shard_map/all_gather | solution.py:49
  628.8 35.8 %copy-start.1 = (bf16[768,256]{1,0:T(8,128)(2,1)S(1)}, bf16[768,256]{1,0:T(8,128)(2,1)}, u32[]{:S(2)}) copy-start(bf16[768,256]{1,0:T(8,128)(2,1)} %all-reduce.11.cloned.1.call-done) | copy-start | bytes 1179652
Sparse Core Ops, SparseCore 0:
  91.8 137.4 all-reduce.4
  231.6 32.3 all-gather.4
  267.1 95.5 all-reduce.6
  364.7 32.3 all-gather.6
  399.9 95.5 all-reduce.8
  497.6 32.3 all-gather.8
  533.2 95.5 all-reduce.10
  630.9 32.3 all-gather.10
where the time goes:
time: 673 us; the launch traced here: 672 us
  waiting for transfers between devices  596 us (89%)
  starting transfers between devices  28 us (4%)
  local copies, waits for them, and re-layouts  19.2 us (3%)
  between operations  13.7 us (2%)
  other arithmetic  9.61 us (1%)
    psum x4, waiting for transfers between devices, spread(): return lax.psum(block, axis)  425 us
    all_gather x4, waiting for transfers between devices, column_panel(): gathered = lax.all_gather(panel[:upper_rows], 'row', axis=0, tiled=True)  131 us
    ppermute x2, waiting for transfers between devices, swapped(): return lax.ppermute(block, axis, route)  20.7 us
    all_to_all x1, waiting for transfers between devices, shards(): lax.all_to_all(buffer, 'row', split_axis=0, concat_axis=0, tiled=True)  19 us
    ppermute x2, starting transfers between devices, swapped(): return lax.ppermute(block, axis, route)  18.3 us
  transfers between devices with their start and end apart: 12, of which 10 were waited for; matrix products, arithmetic and copies ran while one was open for 1% of the time, Pallas kernels for 0%

commit v1 on v0

v1 whole, which is shorter than its diff:
```python
import jax
import jax.numpy as jnp
from jax import lax
from jax.experimental import pallas as pl
from jax.experimental.pallas import tpu as pltpu
from jax.sharding import PartitionSpec as P

MESH = pl.DeviceIdType.MESH
PANELS = 4
F32 = jnp.float32
BF16 = jnp.bfloat16
OWN_ROWS = 1024
LEAD_ROWS = 1280
HOPS = 8


def dot_t(a, b):
    return lax.dot_general(a, b, (((1,), (1,)), ((), ())), preferred_element_type=F32)


def kernel(
    front, winv, contrib, pat, fmap, out,
    cv, fv, wv, sc, cr, own, ys, yr, xs, z, fx, a_st, l_st, part, ox, ob,
    lsem, csend, crecv, ysend, yrecv, xsend, xrecv, fsend, frecv, zsend, zrecv,
    gsend, grecv, tsend, trecv, usend, urecv, qsend, qrecv, vsend, vrecv, osend, orecv,
):
    cube = lax.axis_index("cube")
    row = lax.axis_index("row")
    col = lax.axis_index("col")
    cubes = lax.axis_size("cube")
    core = row % 2
    ylo = row // 2
    half = col // 4
    xpos = col % 4

    def at_row_col(r, c):
        return {"row": r, "col": c}

    core_peer = at_row_col(row ^ 1, col)
    y_peers = {m: at_row_col(row ^ (2 * (m & 1)), col ^ (4 * (m >> 1))) for m in (1, 2, 3)}
    x_peers = {m: at_row_col(row, col ^ m) for m in (1, 2, 3)}
    z_peers = [{"cube": (cube + 1) % cubes}, {"cube": (cube + cubes - 1) % cubes}]

    def remote(src, dst, ssem, rsem, peer):
        return pltpu.make_async_remote_copy(src, dst, ssem, rsem, device_id=peer, device_id_type=MESH)

    loads = [
        pltpu.make_async_copy(contrib, cv, lsem.at[0]),
        pltpu.make_async_copy(front, fv, lsem.at[1]),
        pltpu.make_async_copy(winv, wv, lsem.at[2]),
    ]
    for c in loads:
        c.start()

    barrier = pltpu.get_barrier_semaphore()
    peers = [core_peer, *y_peers.values(), *x_peers.values(), *z_peers]
    for p in peers:
        pl.semaphore_signal(barrier, 1, device_id=p, device_id_type=MESH)
    targets = []
    for s in range(6):
        child = pat[s, 0]
        targets.append(jnp.where(child >= 0, fmap[jnp.maximum(child, 0)], -1))
    loads[0].wait()

    def c_copy(i):
        return remote(sc.at[i], cr.at[i], csend.at[i], crecv.at[i], core_peer)

    for i in range(3):
        def masks(y, c):
            block = y * 2 + c + 4 * i
            return [(t == block).astype(F32) for t in targets]

        away = [masks(y, 1 - core) for y in range(2)]
        stay = [masks(y, core) for y in range(2)]

        def tile(t, carry):
            rows = pl.ds(pl.multiple_of(t * 32, 32), 32)
            vals = [cv[s, rows, :].astype(F32) for s in range(6)]

            def total(ms):
                acc = vals[0] * ms[0]
                for v, m in zip(vals[1:], ms[1:]):
                    acc = acc + v * m
                return acc

            for y in range(2):
                sc[i, y, rows, :] = total(away[y]).astype(BF16)
            for y in range(2):
                own[i, y, rows, :] = total(stay[y])
            return carry

        lax.fori_loop(0, 8, tile, 0)
        if i == 0:
            pl.semaphore_wait(barrier, len(peers))
        c_copy(i).start()

    def y_copy(i):
        return remote(ys.at[i], yr.at[i], ysend.at[i], yrecv.at[i], y_peers[1])

    for i in range(3):
        c_copy(i).wait_recv()
        ys[i] = (own[i, 1 - ylo] + cr[i, 1 - ylo].astype(F32)).astype(BF16)
        y_copy(i).start()
        own[i, ylo] = own[i, ylo] + cr[i, ylo].astype(F32)

    mine = pl.ds(pl.multiple_of(half * 128, 128), 128)
    theirs = pl.ds(pl.multiple_of((1 - half) * 128, 128), 128)

    def x_copy(i):
        return remote(xs.at[i], z.at[half, 0, i], xsend.at[i], xrecv.at[i], y_peers[2])

    def x_arrival(i):
        return remote(xs.at[i], z.at[1 - half, 0, i], xsend.at[i], xrecv.at[i], y_peers[2])

    for i in range(3):
        y_copy(i).wait_recv()
        xs[i] = (own[i, ylo, theirs, :] + yr[i, theirs, :].astype(F32)).astype(BF16)
        x_copy(i).start()
        z[half, 0, i] = (own[i, ylo, mine, :] + yr[i, mine, :].astype(F32)).astype(BF16)

    def z_copy(j, s, i, d):
        rows = pl.ds(d * 64, 64)
        return remote(
            z.at[j, s, i, rows], z.at[j, s + 1, i, rows],
            zsend.at[j, s, i, d], zrecv.at[j, s, i, d], z_peers[d],
        )

    for i in range(3):
        x_arrival(i).wait_recv()
        for d in range(2):
            z_copy(0, 0, i, d).start()

    loads[1].wait()
    f_copy = remote(fv.at[:, theirs], fx, fsend, frecv, y_peers[2])
    f_copy.start()

    def z_step(j, s):
        for i in range(3):
            for d in range(2):
                z_copy(j, s - 1, i, d).wait_recv()
                z_copy(j, s, i, d).start()

    def z_body(s, carry):
        z_step(0, s)
        return carry

    lax.fori_loop(1, HOPS, z_body, 0)
    for i in range(3):
        for d in range(2):
            z_copy(1, 0, i, d).start()

    top = pl.multiple_of(row * 256 + half * 128, 128)
    f_copy.wait_recv()
    first = half == 0

    def g_copy(m, part_no):
        rows = pl.ds(top, 128) if part_no == 0 else pl.ds(OWN_ROWS, 256)
        ref = a_st.at[xpos, rows]
        return remote(ref, ref, gsend.at[m - 1, part_no], grecv.at[m - 1, part_no], x_peers[m])

    def g_arrival(m, part_no):
        rows = pl.ds(top, 128) if part_no == 0 else pl.ds(OWN_ROWS, 256)
        ref = a_st.at[xpos ^ m, rows]
        return remote(ref, ref, gsend.at[m - 1, part_no], grecv.at[m - 1, part_no], x_peers[m])

    for i in range(3):
        for d in range(2):
            z_copy(0, HOPS - 1, i, d).wait_recv()
        base = jnp.where(first, fv[i, mine, :].astype(F32), fx[i].astype(F32))
        value = (base + z[0, HOPS, i].astype(F32)).astype(BF16)
        if i == 0:
            a_st[xpos, pl.ds(top, 128), :] = value
            for m in (1, 2, 3):
                g_copy(m, 0).start()
        else:
            a_st[xpos, pl.ds(OWN_ROWS + (i - 1) * 128, 128), :] = value
    for m in (1, 2, 3):
        g_copy(m, 1).start()

    for k in range(PANELS):
        @pl.when(row <= k)
        def _():
            l_st[k, pl.ds(top, 128), :] = jnp.zeros((128, 256), BF16)

    z_step(1, 1)
    z_step(1, 2)

    def tri_place(r, h):
        return a_st.at[pl.ds(0, 3), pl.ds(pl.multiple_of(r * 256 + h * 128, 128), 128)]

    def lead_place(h):
        return a_st.at[:, pl.ds(pl.multiple_of(LEAD_ROWS + h * 128, 128), 128)]

    def owner(m):
        return row ^ (2 * (m & 1)), half ^ (m >> 1)

    def t_copy(m):
        ref = tri_place(row, half)
        return remote(ref, ref, tsend.at[m - 1], trecv.at[m - 1], y_peers[m])

    def t_arrival(m):
        ref = tri_place(*owner(m))
        return remote(ref, ref, tsend.at[m - 1], trecv.at[m - 1], y_peers[m])

    def u_copy(m):
        ref = tri_place(*owner(m))
        return remote(ref, ref, usend.at[m], urecv.at[m], core_peer)

    def u_arrival(m):
        r, h = owner(m)
        ref = tri_place(r ^ 1, h)
        return remote(ref, ref, usend.at[m], urecv.at[m], core_peer)

    def q_copy(m):
        return remote(lead_place(half), lead_place(half), qsend.at[m - 1], qrecv.at[m - 1], y_peers[m])

    def q_arrival(m):
        ref = lead_place(owner(m)[1])
        return remote(ref, ref, qsend.at[m - 1], qrecv.at[m - 1], y_peers[m])

    def v_copy(m):
        ref = lead_place(owner(m)[1])
        return remote(ref, ref, vsend.at[m], vrecv.at[m], core_peer)

    for m in (1, 2, 3):
        for part_no in range(2):
            g_arrival(m, part_no).wait_recv()
    for m in (1, 2, 3):
        t_copy(m).start()
    u_copy(0).start()

    @pl.when(row == xpos)
    def _():
        for k in range(4):
            a_st[k, pl.ds(pl.multiple_of(LEAD_ROWS + half * 128, 128), 128), :] = a_st[k, pl.ds(OWN_ROWS, 128), :]
        for m in (1, 2, 3):
            q_copy(m).start()
        v_copy(0).start()

    z_step(1, 3)
    z_step(1, 4)

    for m in (1, 2, 3):
        t_arrival(m).wait_recv()
        u_copy(m).start()

        @pl.when(owner(m)[0] == xpos)
        def _():
            q_arrival(m).wait_recv()
            v_copy(m).start()

    z_step(1, 5)

    for m in range(4):
        u_arrival(m).wait_recv()

        @pl.when((owner(m)[0] ^ 1) == xpos)
        def _():
            v_copy(m).wait_recv()

    loads[2].wait()

    def panel(k, b):
        rows = pl.ds(b * 256, 256)
        acc = a_st[k, rows, :].astype(F32)
        for m in range(k):
            acc = acc - dot_t(l_st[m, rows, :], l_st[m, pl.ds(k * 256, 256), :])
        weight = wv[pl.ds(k * 256, 256), :]
        l_st[k, rows, :] = jnp.dot(acc.astype(BF16), weight, preferred_element_type=F32).astype(BF16)

    for k in range(2):
        for b in range(k + 1, 6):
            panel(k, b)
    z_step(1, 6)
    for k in range(2, 4):
        for b in range(k + 1, 6):
            panel(k, b)
    z_step(1, 7)

    def rows_of(i):
        return pl.ds(top, 128) if i == 0 else pl.ds(OWN_ROWS + (i - 1) * 128, 128)

    for i in range(3):
        acc = jnp.where(first, fx[i].astype(F32), fv[i, mine, :].astype(F32))
        for k in range(PANELS):
            acc = acc - dot_t(l_st[k, rows_of(i), :], l_st[k, pl.ds(LEAD_ROWS, 256), :])
        part[i] = acc

    def o_copy(i):
        return remote(ox.at[i], ob.at[i, mine], osend.at[i], orecv.at[i], y_peers[2])

    def o_arrival(i):
        return remote(ox.at[i], ob.at[i, theirs], osend.at[i], orecv.at[i], y_peers[2])

    for i in range(3):
        for d in range(2):
            z_copy(1, HOPS - 1, i, d).wait_recv()
        late = (part[i] + z[1, HOPS, i].astype(F32)).astype(BF16)
        early = l_st[xpos, rows_of(i), :]
        ox[i] = jnp.where(first, late, early)
        o_copy(i).start()
        ob[i, mine, :] = jnp.where(first, early, late)
    for i in range(3):
        o_arrival(i).wait_recv()
    store = pltpu.make_async_copy(ob, out, lsem.at[3])
    store.start()

    for i in range(3):
        c_copy(i).wait_send()
        y_copy(i).wait_send()
        x_copy(i).wait_send()
        o_copy(i).wait_send()
    f_copy.wait_send()
    for m in (1, 2, 3):
        for part_no in range(2):
            g_copy(m, part_no).wait_send()
        t_copy(m).wait_send()
    for m in range(4):
        u_copy(m).wait_send()

        @pl.when(owner(m)[0] == xpos)
        def _():
            v_copy(m).wait_send()

    @pl.when(row == xpos)
    def _():
        for m in (1, 2, 3):
            q_copy(m).wait_send()

    def drain(s, carry):
        for j in range(2):
            for i in range(3):
                for d in range(2):
                    z_copy(j, s, i, d).wait_send()
        return carry

    lax.fori_loop(0, HOPS, drain, 0)
    store.wait()


def shards(front, panel_inverse, contrib, pattern, front_map):
    hbm = pl.BlockSpec(memory_space=pl.ANY)
    smem = pl.BlockSpec(memory_space=pltpu.SMEM)

    def vmem(*shape, dtype=BF16):
        return pltpu.VMEM(shape, dtype)

    def dma(*shape):
        return pltpu.SemaphoreType.DMA(shape)

    out = pl.pallas_call(
        kernel,
        out_shape=jax.ShapeDtypeStruct((3, 256, 256), BF16),
        in_specs=[hbm, hbm, hbm, smem, smem],
        out_specs=hbm,
        scratch_shapes=[
            vmem(6, 256, 256),
            vmem(3, 256, 256),
            vmem(1024, 256),
            vmem(3, 2, 256, 256),
            vmem(3, 2, 256, 256),
            vmem(3, 2, 256, 256, dtype=F32),
            vmem(3, 256, 256),
            vmem(3, 256, 256),
            vmem(3, 128, 256),
            vmem(2, HOPS + 1, 3, 128, 256),
            vmem(3, 128, 256),
            vmem(4, 1536, 256),
            vmem(4, 1536, 256),
            vmem(3, 128, 256, dtype=F32),
            vmem(3, 128, 256),
            vmem(3, 256, 256),
            dma(4),
            dma(3), dma(3), dma(3), dma(3), dma(3), dma(3),
            pltpu.SemaphoreType.DMA, pltpu.SemaphoreType.DMA,
            dma(2, HOPS, 3, 2), dma(2, HOPS, 3, 2),
            dma(3, 2), dma(3, 2),
            dma(3), dma(3), dma(4), dma(4),
            dma(3), dma(3), dma(4), dma(4),
            dma(3), dma(3),
        ],
        compiler_params=pltpu.CompilerParams(
            collective_id=0, has_side_effects=True, vmem_limit_bytes=60 * 2**20
        ),
        name="extend_add_eliminate",
    )(front.reshape(3, 256, 256), panel_inverse[0], contrib[0], pattern[0], front_map[0])
    return out.reshape(1, 768, 256)


def solution(mesh):
    in_specs = (
        P("cube", "row", "col"),
        P("cube", None, None),
        P("cube", ("row", "col"), None, None),
        P("cube", ("row", "col"), None),
        P("cube", None),
    )
    out_specs = P("cube", "row", "col")
    return jax.shard_map(shards, mesh=mesh, in_specs=in_specs, out_specs=out_specs, check_vma=False)
```

time: 673 us -> 97.4 us (0.14)
  the two profiles are of different devices: /device:TPU:1 before, /device:TPU:16 now
where the time goes in v1:
time: 97.4 us; the launch traced here: 97.2 us
  Pallas kernels  94.1 us (97%)
  local copies, waits for them, and re-layouts  3.12 us (3%)
    pallas_call x1, Pallas kernels, shards(): pl.pallas_call(kernel, out_shape=jax.ShapeDtypeStruct((3, 256, 256), BF16...  94.1 us
    unnamed x3, local copies, waits for them, and re-layouts  2.45 us

profile of v1, /device:TPU:16, one launch (start us, length us, event | category | flops | bytes accessed | tf_op | source)
XLA Modules:
  0.0 97.2 jit_solution(12512842643292510931)
XLA Ops:
  0.0 0.0 copy-start
  0.0 0.7 copy-done
  0.7 0.7 copy.6.pat
  1.4 94.1 %extend_add_eliminate.1 = bf16[3,256,256]{2,1,0:T(8,128)(2,1)} custom-call(bf16[3,256,256]{2,1,0:T(8,128)(2,1)} %bitcast.9, bf16[1024,256]{1,0:T(8,128)(2,1)} %bitcast.8, bf16[6,256,256]{2,1,0:T(8,128)(2,1)} %bitcast.7, s32[6,2]{1,0:T(8,128)} %copy.6.pat, s32[12]{0:T(128)} %bitcast.11), custom_call_target="tpu_custom_call" | custom-call | tf_op jit(solution)/shard_map/extend_add_eliminate/pallas_call | solution.py:351
  95.4 1.8 %copy.8 = bf16[1,768,256]{2,1,0:T(8,128)(2,1)} copy(bf16[1,768,256]{2,1,0:T(8,128)(2,1)} %bitcast.6) | data formatting | bytes 786432
Async XLA Ops:
  0.0 0.7 copy-start

commit v2 on v1

v2 whole, which is shorter than its diff:
```python
import jax
import jax.numpy as jnp
from jax import lax
from jax.experimental import pallas as pl
from jax.experimental.pallas import tpu as pltpu
from jax.sharding import PartitionSpec as P

MESH = pl.DeviceIdType.MESH
PANELS = 4
F32 = jnp.float32
BF16 = jnp.bfloat16
OWN_ROWS = 1024
LEAD_ROWS = 1280


def dot_t(a, b):
    return lax.dot_general(a, b, (((1,), (1,)), ((), ())), preferred_element_type=F32)


def kernel(
    front, winv, contrib, pat, fmap, out,
    cv, fv, wv, sc, cr, own, kept, ys, yr, zs, zr, fx, a_st, l_st, part, ox, ob,
    lsem, csend, crecv, ysend, yrecv, fsend, frecv, zsend, zrecv,
    gsend, grecv, tsend, trecv, usend, urecv, qsend, qrecv, vsend, vrecv, osend, orecv,
):
    cube = lax.axis_index("cube")
    row = lax.axis_index("row")
    col = lax.axis_index("col")
    cubes = lax.axis_size("cube")
    core = row % 2
    ylo = row // 2
    half = col // 4
    xpos = col % 4

    def at_row_col(r, c):
        return {"row": r, "col": c}

    core_peer = at_row_col(row ^ 1, col)
    y_peers = {m: at_row_col(row ^ (2 * (m & 1)), col ^ (4 * (m >> 1))) for m in (1, 2, 3)}
    x_peers = {m: at_row_col(row, col ^ m) for m in (1, 2, 3)}
    z_peer = {"cube": (cube + cubes // 2) % cubes}

    def remote(src, dst, ssem, rsem, peer):
        return pltpu.make_async_remote_copy(src, dst, ssem, rsem, device_id=peer, device_id_type=MESH)

    barrier = pltpu.get_barrier_semaphore()
    peers = [z_peer, core_peer, *y_peers.values(), *x_peers.values()]
    for p in peers:
        pl.semaphore_signal(barrier, 1, device_id=p, device_id_type=MESH)
    loads = [
        pltpu.make_async_copy(contrib, cv, lsem.at[0]),
        pltpu.make_async_copy(front, fv, lsem.at[1]),
        pltpu.make_async_copy(winv, wv, lsem.at[2]),
    ]
    for c in loads:
        c.start()

    targets = []
    for s in range(6):
        child = pat[0, s]
        targets.append(jnp.where(child >= 0, fmap[jnp.maximum(child, 0)], -1))
    loads[0].wait()

    def c_copy(i):
        return remote(sc.at[i], cr.at[i], csend.at[i], crecv.at[i], core_peer)

    for i in range(3):
        def masks(y, c):
            block = y * 2 + c + 4 * i
            return [(t == block).astype(F32) for t in targets]

        away = [masks(y, 1 - core) for y in range(2)]
        stay = [masks(y, core) for y in range(2)]

        def tile(t, carry):
            rows = pl.ds(pl.multiple_of(t * 32, 32), 32)
            vals = [cv[s, rows, :].astype(F32) for s in range(6)]

            def total(ms):
                acc = vals[0] * ms[0]
                for v, m in zip(vals[1:], ms[1:]):
                    acc = acc + v * m
                return acc

            for y in range(2):
                sc[i, y, rows, :] = total(away[y]).astype(BF16)
            for y in range(2):
                own[i, y, rows, :] = total(stay[y])
            return carry

        lax.fori_loop(0, 8, tile, 0)

    pl.semaphore_wait(barrier, len(peers))
    for i in range(3):
        c_copy(i).start()

    own_half = pl.ds(pl.multiple_of(half * 128, 128), 128)
    far_half = pl.ds(pl.multiple_of((1 - half) * 128, 128), 128)

    def y_copy(m, i):
        return remote(ys.at[m - 1, i], yr.at[m - 1, i], ysend.at[m - 1, i], yrecv.at[m - 1, i], y_peers[m])

    def both(i, y, rows):
        return own[i, y, rows, :] + cr[i, y, rows, :].astype(F32)

    for i in range(3):
        c_copy(i).wait_recv()
        ys[2, i] = both(i, 1 - ylo, far_half).astype(BF16)
        y_copy(3, i).start()
        ys[1, i] = both(i, ylo, far_half).astype(BF16)
        y_copy(2, i).start()
        ys[0, i] = both(i, 1 - ylo, own_half).astype(BF16)
        y_copy(1, i).start()
        kept[i] = both(i, ylo, own_half)

    def z_copy(j, i):
        return remote(zs.at[j, i], zr.at[j, i], zsend.at[j, i], zrecv.at[j, i], z_peer)

    for i in range(3):
        for m in (1, 2, 3):
            y_copy(m, i).wait_recv()
        zs[half, i] = (kept[i] + yr[0, i].astype(F32)).astype(BF16)
        zs[1 - half, i] = (yr[1, i].astype(F32) + yr[2, i].astype(F32)).astype(BF16)
        z_copy(0, i).start()

    loads[1].wait()
    f_copy = remote(fv.at[:, far_half], fx, fsend, frecv, y_peers[2])
    f_copy.start()

    top = pl.multiple_of(row * 256 + half * 128, 128)

    def rows_of(i):
        return pl.ds(top, 128) if i == 0 else pl.ds(OWN_ROWS + (i - 1) * 128, 128)

    for k in range(PANELS):
        @pl.when(row <= k)
        def _():
            l_st[k, rows_of(0), :] = jnp.zeros((128, 256), BF16)

    f_copy.wait_recv()
    first = half == 0

    def g_copy(m, i):
        ref = a_st.at[xpos, rows_of(i)]
        return remote(ref, ref, gsend.at[m - 1, i], grecv.at[m - 1, i], x_peers[m])

    def g_arrival(m, i):
        ref = a_st.at[xpos ^ m, rows_of(i)]
        return remote(ref, ref, gsend.at[m - 1, i], grecv.at[m - 1, i], x_peers[m])

    def critical(i):
        z_copy(0, i).wait_recv()
        base = jnp.where(first, fv[i, own_half, :].astype(F32), fx[i].astype(F32))
        a_st[xpos, rows_of(i), :] = (base + zr[0, i].astype(F32)).astype(BF16)

    def owner(m):
        return row ^ (2 * (m & 1)), half ^ (m >> 1)

    def tri_place(k, r, h):
        return a_st.at[k, pl.ds(pl.multiple_of(r * 256 + h * 128, 128), 128)]

    def lead_place(h):
        return a_st.at[:, pl.ds(pl.multiple_of(LEAD_ROWS + h * 128, 128), 128)]

    def t_copy(m, k):
        ref = tri_place(k, row, half)
        return remote(ref, ref, tsend.at[m - 1, k], trecv.at[m - 1, k], y_peers[m])

    def t_arrival(m, k):
        ref = tri_place(k, *owner(m))
        return remote(ref, ref, tsend.at[m - 1, k], trecv.at[m - 1, k], y_peers[m])

    def u_copy(m, k):
        ref = tri_place(k, *owner(m))
        return remote(ref, ref, usend.at[m, k], urecv.at[m, k], core_peer)

    def u_arrival(m, k):
        r, h = owner(m)
        ref = tri_place(k, r ^ 1, h)
        return remote(ref, ref, usend.at[m, k], urecv.at[m, k], core_peer)

    def q_copy(m):
        return remote(lead_place(half), lead_place(half), qsend.at[m - 1], qrecv.at[m - 1], y_peers[m])

    def q_arrival(m):
        ref = lead_place(owner(m)[1])
        return remote(ref, ref, qsend.at[m - 1], qrecv.at[m - 1], y_peers[m])

    def v_copy(m):
        ref = lead_place(owner(m)[1])
        return remote(ref, ref, vsend.at[m], vrecv.at[m], core_peer)

    def each(count, body):
        def step(k, carry):
            body(k)
            return carry

        lax.fori_loop(0, count, step, 0)

    critical(0)

    @pl.when(row > xpos)
    def _():
        for m in (1, 2, 3):
            g_copy(m, 0).start()

    z_copy(1, 0).start()
    critical(1)
    for m in (1, 2, 3):
        g_copy(m, 1).start()
    z_copy(1, 1).start()
    for m in (1, 2, 3):
        @pl.when(row > (xpos ^ m))
        def _():
            g_arrival(m, 0).wait_recv()

    def send_tri(k):
        for m in (3, 1, 2):
            t_copy(m, k).start()
        u_copy(0, k).start()

    each(row, send_tri)

    for m in (1, 2, 3):
        g_arrival(m, 1).wait_recv()

    @pl.when(row == xpos)
    def _():
        for k in range(4):
            a_st[k, pl.ds(pl.multiple_of(LEAD_ROWS + half * 128, 128), 128), :] = a_st[k, rows_of(1), :]
        for m in (3, 1, 2):
            q_copy(m).start()
        v_copy(0).start()

    critical(2)
    for m in (1, 2, 3):
        g_copy(m, 2).start()
    z_copy(1, 2).start()

    for m in (1, 3, 2):
        def relay_tri(k):
            t_arrival(m, k).wait_recv()
            u_copy(m, k).start()

        each(owner(m)[0], relay_tri)
    for m in (1, 3, 2):
        @pl.when(owner(m)[0] == xpos)
        def _():
            q_arrival(m).wait_recv()
            v_copy(m).start()

    for m in range(4):
        each(owner(m)[0] ^ 1, lambda k: u_arrival(m, k).wait_recv())
    loads[2].wait()

    def panel(k, b):
        rows = pl.ds(b * 256, 256)
        acc = a_st[k, rows, :].astype(F32)
        for m in range(k):
            acc = acc - dot_t(l_st[m, rows, :], l_st[m, pl.ds(k * 256, 256), :])
        weight = wv[pl.ds(k * 256, 256), :]
        l_st[k, rows, :] = jnp.dot(acc.astype(BF16), weight, preferred_element_type=F32).astype(BF16)

    for k in range(3):
        for b in range(k + 1, 4):
            panel(k, b)
    for m in (1, 2, 3):
        g_arrival(m, 2).wait_recv()
    for k in range(PANELS):
        panel(k, 4)
    for m in range(4):
        @pl.when((owner(m)[0] ^ 1) == xpos)
        def _():
            v_copy(m).wait_recv()

    for k in range(PANELS):
        panel(k, 5)

    for i in range(3):
        acc = jnp.where(first, fx[i].astype(F32), fv[i, own_half, :].astype(F32))
        for k in range(PANELS):
            acc = acc - dot_t(l_st[k, rows_of(i), :], l_st[k, pl.ds(LEAD_ROWS, 256), :])
        part[i] = acc

    def o_copy(i):
        return remote(ox.at[i], ob.at[i, own_half], osend.at[i], orecv.at[i], y_peers[2])

    def o_arrival(i):
        return remote(ox.at[i], ob.at[i, far_half], osend.at[i], orecv.at[i], y_peers[2])

    for i in range(3):
        z_copy(1, i).wait_recv()
        late = (part[i] + zr[1, i].astype(F32)).astype(BF16)
        early = l_st[xpos, rows_of(i), :]
        ox[i] = jnp.where(first, late, early)
        o_copy(i).start()
        ob[i, own_half, :] = jnp.where(first, early, late)
    for i in range(3):
        o_arrival(i).wait_recv()
    store = pltpu.make_async_copy(ob, out, lsem.at[3])
    store.start()

    f_copy.wait_send()
    for i in range(3):
        c_copy(i).wait_send()
        o_copy(i).wait_send()
        for m in (1, 2, 3):
            y_copy(m, i).wait_send()
            if i:
                g_copy(m, i).wait_send()

    @pl.when(row > xpos)
    def _():
        for m in (1, 2, 3):
            g_copy(m, 0).wait_send()

    def drain_tri(k):
        for m in (1, 2, 3):
            t_copy(m, k).wait_send()

    each(row, drain_tri)
    for m in range(4):
        each(owner(m)[0], lambda k: u_copy(m, k).wait_send())

        @pl.when(owner(m)[0] == xpos)
        def _():
            v_copy(m).wait_send()

    @pl.when(row == xpos)
    def _():
        for m in (1, 2, 3):
            q_copy(m).wait_send()

    for i in range(3):
        for j in range(2):
            z_copy(j, i).wait_send()
    store.wait()


def shards(front, panel_inverse, contrib, pattern, front_map):
    hbm = pl.BlockSpec(memory_space=pl.ANY)
    smem = pl.BlockSpec(memory_space=pltpu.SMEM)

    def vmem(*shape, dtype=BF16):
        return pltpu.VMEM(shape, dtype)

    def dma(*shape):
        return pltpu.SemaphoreType.DMA(shape)

    out = pl.pallas_call(
        kernel,
        out_shape=jax.ShapeDtypeStruct((3, 256, 256), BF16),
        in_specs=[hbm, hbm, hbm, smem, smem],
        out_specs=hbm,
        scratch_shapes=[
            vmem(6, 256, 256),
            vmem(3, 256, 256),
            vmem(1024, 256),
            vmem(3, 2, 256, 256),
            vmem(3, 2, 256, 256),
            vmem(3, 2, 256, 256, dtype=F32),
            vmem(3, 128, 256, dtype=F32),
            vmem(3, 3, 128, 256),
            vmem(3, 3, 128, 256),
            vmem(2, 3, 128, 256),
            vmem(2, 3, 128, 256),
            vmem(3, 128, 256),
            vmem(4, 1536, 256),
            vmem(4, 1536, 256),
            vmem(3, 128, 256, dtype=F32),
            vmem(3, 128, 256),
            vmem(3, 256, 256),
            dma(4),
            dma(3), dma(3), dma(3, 3), dma(3, 3),
            pltpu.SemaphoreType.DMA, pltpu.SemaphoreType.DMA,
            dma(2, 3), dma(2, 3),
            dma(3, 3), dma(3, 3),
            dma(3, 3), dma(3, 3), dma(4, 3), dma(4, 3),
            dma(3), dma(3), dma(4), dma(4),
            dma(3), dma(3),
        ],
        compiler_params=pltpu.CompilerParams(
            collective_id=0, has_side_effects=True, vmem_limit_bytes=60 * 2**20
        ),
        name="extend_add_eliminate",
    )(front.reshape(3, 256, 256), panel_inverse[0], contrib[0], pattern[0].T, front_map[0])
    return out.reshape(1, 768, 256)


def solution(mesh):
    in_specs = (
        P("cube", "row", "col"),
        P("cube", None, None),
        P("cube", ("row", "col"), None, None),
        P("cube", ("row", "col"), None),
        P("cube", None),
    )
    out_specs = P("cube", "row", "col")
    return jax.shard_map(shards, mesh=mesh, in_specs=in_specs, out_specs=out_specs, check_vma=False)
```

time: 97.4 us -> 74.4 us (0.76)
  the two profiles are of different devices: /device:TPU:16 before, /device:TPU:32 now
where the time goes in v2:
time: 74.4 us; the launch traced here: 74.2 us
  Pallas kernels  72.4 us (97%)
  local copies, waits for them, and re-layouts  1.77 us (2%)
    pallas_call x1, Pallas kernels, shards(): pl.pallas_call(kernel, out_shape=jax.ShapeDtypeStruct((3, 256, 256), BF16...  72.4 us
    unnamed x1, local copies, waits for them, and re-layouts  1.77 us

profile of v2, /device:TPU:32, one launch (start us, length us, event | category | flops | bytes accessed | tf_op | source)
XLA Modules:
  0.0 74.2 jit_solution(16851450113566829195)
XLA Ops:
  0.0 72.4 %extend_add_eliminate.1 = bf16[3,256,256]{2,1,0:T(8,128)(2,1)} custom-call(bf16[3,256,256]{2,1,0:T(8,128)(2,1)} %bitcast.11, bf16[1024,256]{1,0:T(8,128)(2,1)} %bitcast.10, bf16[6,256,256]{2,1,0:T(8,128)(2,1)} %bitcast.9, s32[2,6]{1,0:T(2,128)} %bitcast.12, s32[12]{0:T(128)} %bitcast.13), custom_call_target="tpu_custom_call" | custom-call | tf_op jit(solution)/shard_map/extend_add_eliminate/pallas_call | solution.py:350
  72.4 1.8 %copy.7 = bf16[1,768,256]{2,1,0:T(8,128)(2,1)} copy(bf16[1,768,256]{2,1,0:T(8,128)(2,1)} %bitcast.8) | data formatting | bytes 786432

commit v3 on v2

--- a/solution.py
+++ b/solution.py
@@ -11,6 +11,7 @@
 BF16 = jnp.bfloat16
 OWN_ROWS = 1024
 LEAD_ROWS = 1280
+ORDER = (1, 0, 2)
 
 
 def dot_t(a, b):
@@ -19,7 +20,7 @@
 
 def kernel(
     front, winv, contrib, pat, fmap, out,
-    cv, fv, wv, sc, cr, own, kept, ys, yr, zs, zr, fx, a_st, l_st, part, ox, ob,
+    cv, fv, wv, sc, cr, own, kept, ys, yr, zs, zr, fx, a_st, l_st, ox, ob,
     lsem, csend, crecv, ysend, yrecv, fsend, frecv, zsend, zrecv,
     gsend, grecv, tsend, trecv, usend, urecv, qsend, qrecv, vsend, vrecv, osend, orecv,
 ):
@@ -64,7 +65,7 @@
     def c_copy(i):
         return remote(sc.at[i], cr.at[i], csend.at[i], crecv.at[i], core_peer)
 
-    for i in range(3):
+    for i in ORDER:
         def masks(y, c):
             block = y * 2 + c + 4 * i
             return [(t == block).astype(F32) for t in targets]
@@ -91,7 +92,7 @@
         lax.fori_loop(0, 8, tile, 0)
 
     pl.semaphore_wait(barrier, len(peers))
-    for i in range(3):
+    for i in ORDER:
         c_copy(i).start()
 
     own_half = pl.ds(pl.multiple_of(half * 128, 128), 128)
@@ -103,8 +104,11 @@
     def both(i, y, rows):
         return own[i, y, rows, :] + cr[i, y, rows, :].astype(F32)
 
-    for i in range(3):
+    for n, i in enumerate(ORDER):
         c_copy(i).wait_recv()
+        if n:
+            for m in (1, 2, 3):
+                y_copy(m, ORDER[n - 1]).wait_send()
         ys[2, i] = both(i, 1 - ylo, far_half).astype(BF16)
         y_copy(3, i).start()
         ys[1, i] = both(i, ylo, far_half).astype(BF16)
@@ -116,7 +120,7 @@
     def z_copy(j, i):
         return remote(zs.at[j, i], zr.at[j, i], zsend.at[j, i], zrecv.at[j, i], z_peer)
 
-    for i in range(3):
+    for i in ORDER:
         for m in (1, 2, 3):
             y_copy(m, i).wait_recv()
         zs[half, i] = (kept[i] + yr[0, i].astype(F32)).astype(BF16)
@@ -180,7 +184,8 @@
         return remote(ref, ref, usend.at[m, k], urecv.at[m, k], core_peer)
 
     def q_copy(m):
-        return remote(lead_place(half), lead_place(half), qsend.at[m - 1], qrecv.at[m - 1], y_peers[m])
+        src = a_st.at[:, rows_of(1)]
+        return remote(src, lead_place(half), qsend.at[m - 1], qrecv.at[m - 1], y_peers[m])
 
     def q_arrival(m):
         ref = lead_place(owner(m)[1])
@@ -188,7 +193,8 @@
 
     def v_copy(m):
         ref = lead_place(owner(m)[1])
-        return remote(ref, ref, vsend.at[m], vrecv.at[m], core_peer)
+        src = a_st.at[:, rows_of(1)] if m == 0 else ref
+        return remote(src, ref, vsend.at[m], vrecv.at[m], core_peer)
 
     def each(count, body):
         def step(k, carry):
@@ -197,18 +203,31 @@
 
         lax.fori_loop(0, count, step, 0)
 
-    critical(0)
-
-    @pl.when(row > xpos)
-    def _():
-        for m in (1, 2, 3):
-            g_copy(m, 0).start()
-
-    z_copy(1, 0).start()
     critical(1)
     for m in (1, 2, 3):
         g_copy(m, 1).start()
+    z_copy(1, 0).start()
+
+    critical(0)
+
+    @pl.when(row > xpos)
+    def _():
+        for m in (1, 2, 3):
+            g_copy(m, 0).start()
+
     z_copy(1, 1).start()
+
+    for m in (1, 2, 3):
+        g_arrival(m, 1).wait_recv()
+
+    @pl.when(row == xpos)
+    def _():
+        for m in (3, 1, 2):
+            q_copy(m).start()
+        v_copy(0).start()
+        for k in range(4):
+            a_st[k, pl.ds(pl.multiple_of(LEAD_ROWS + half * 128, 128), 128), :] = a_st[k, rows_of(1), :]
+
     for m in (1, 2, 3):
         @pl.when(row > (xpos ^ m))
         def _():
@@ -221,34 +240,22 @@
 
     each(row, send_tri)
 
-    for m in (1, 2, 3):
-        g_arrival(m, 1).wait_recv()
-
-    @pl.when(row == xpos)
-    def _():
-        for k in range(4):
-            a_st[k, pl.ds(pl.multiple_of(LEAD_ROWS + half * 128, 128), 128), :] = a_st[k, rows_of(1), :]
-        for m in (3, 1, 2):
-            q_copy(m).start()
-        v_copy(0).start()
-
     critical(2)
     for m in (1, 2, 3):
         g_copy(m, 2).start()
     z_copy(1, 2).start()
 
     for m in (1, 3, 2):
+        @pl.when(owner(m)[0] == xpos)
+        def _():
+            q_arrival(m).wait_recv()
+            v_copy(m).start()
+    for m in (1, 3, 2):
         def relay_tri(k):
             t_arrival(m, k).wait_recv()
             u_copy(m, k).start()
 
         each(owner(m)[0], relay_tri)
-    for m in (1, 3, 2):
-        @pl.when(owner(m)[0] == xpos)
-        def _():
-            q_arrival(m).wait_recv()
-            v_copy(m).start()
-
     for m in range(4):
         each(owner(m)[0] ^ 1, lambda k: u_arrival(m, k).wait_recv())
     loads[2].wait()
@@ -268,6 +275,28 @@
         g_arrival(m, 2).wait_recv()
     for k in range(PANELS):
         panel(k, 4)
+    def o_copy(i):
+        return remote(ox.at[i], out.at[i, own_half], osend.at[i], orecv.at[i], y_peers[2])
+
+    def keep_copy(i):
+        return pltpu.make_async_copy(ob.at[i], out.at[i, own_half], lsem.at[3 + i])
+
+    def o_arrival(i):
+        return remote(ox.at[i], out.at[i, far_half], osend.at[i], orecv.at[i], y_peers[2])
+
+    for i in range(3):
+        early = l_st[xpos, rows_of(i), :]
+
+        @pl.when(first)
+        def _():
+            ob[i] = early
+            keep_copy(i).start()
+
+        @pl.when(jnp.logical_not(first))
+        def _():
+            ox[i] = early
+            o_copy(i).start()
+
     for m in range(4):
         @pl.when((owner(m)[0] ^ 1) == xpos)
         def _():
@@ -280,32 +309,29 @@
         acc = jnp.where(first, fx[i].astype(F32), fv[i, own_half, :].astype(F32))
         for k in range(PANELS):
             acc = acc - dot_t(l_st[k, rows_of(i), :], l_st[k, pl.ds(LEAD_ROWS, 256), :])
-        part[i] = acc
-
-    def o_copy(i):
-        return remote(ox.at[i], ob.at[i, own_half], osend.at[i], orecv.at[i], y_peers[2])
-
-    def o_arrival(i):
-        return remote(ox.at[i], ob.at[i, far_half], osend.at[i], orecv.at[i], y_peers[2])
-
-    for i in range(3):
         z_copy(1, i).wait_recv()
-        late = (part[i] + zr[1, i].astype(F32)).astype(BF16)
-        early = l_st[xpos, rows_of(i), :]
-        ox[i] = jnp.where(first, late, early)
-        o_copy(i).start()
-        ob[i, own_half, :] = jnp.where(first, early, late)
+        late = (acc + zr[1, i].astype(F32)).astype(BF16)
+
+        @pl.when(first)
+        def _():
+            ox[i] = late
+            o_copy(i).start()
+
+        @pl.when(jnp.logical_not(first))
+        def _():
+            ob[i] = late
+            keep_copy(i).start()
+
     for i in range(3):
         o_arrival(i).wait_recv()
-    store = pltpu.make_async_copy(ob, out, lsem.at[3])
-    store.start()
 
     f_copy.wait_send()
     for i in range(3):
         c_copy(i).wait_send()
         o_copy(i).wait_send()
         for m in (1, 2, 3):
-            y_copy(m, i).wait_send()
+            if i == ORDER[-1]:
+                y_copy(m, i).wait_send()
             if i:
                 g_copy(m, i).wait_send()
 
@@ -334,7 +360,8 @@
     for i in range(3):
         for j in range(2):
             z_copy(j, i).wait_send()
-    store.wait()
+    for i in range(3):
+        keep_copy(i).wait()
 
 
 def shards(front, panel_inverse, contrib, pattern, front_map):
@@ -367,10 +394,9 @@
             vmem(3, 128, 256),
             vmem(4, 1536, 256),
             vmem(4, 1536, 256),
-            vmem(3, 128, 256, dtype=F32),
             vmem(3, 128, 256),
-            vmem(3, 256, 256),
-            dma(4),
+            vmem(3, 128, 256),
+            dma(6),
             dma(3), dma(3), dma(3, 3), dma(3, 3),
             pltpu.SemaphoreType.DMA, pltpu.SemaphoreType.DMA,
             dma(2, 3), dma(2, 3),

time: 74.4 us -> 70.2 us (0.944)
  the two profiles are of different devices: /device:TPU:32 before, /device:TPU:93 now
where the time goes in v3:
time: 70.2 us; the launch traced here: 70 us
  Pallas kernels  68.3 us (97%)
  local copies, waits for them, and re-layouts  1.77 us (3%)
    pallas_call x1, Pallas kernels, shards(): pl.pallas_call(kernel, out_shape=jax.ShapeDtypeStruct((3, 256, 256), BF16...  68.3 us
    unnamed x1, local copies, waits for them, and re-layouts  1.77 us

profile of v3, /device:TPU:93, one launch (start us, length us, event | category | flops | bytes accessed | tf_op | source)
XLA Modules:
  0.0 70.0 jit_solution(16360169150176209469)
XLA Ops:
  0.0 68.3 %extend_add_eliminate.1 = bf16[3,256,256]{2,1,0:T(8,128)(2,1)} custom-call(bf16[3,256,256]{2,1,0:T(8,128)(2,1)} %bitcast.11, bf16[1024,256]{1,0:T(8,128)(2,1)} %bitcast.10, bf16[6,256,256]{2,1,0:T(8,128)(2,1)} %bitcast.9, s32[2,6]{1,0:T(2,128)} %bitcast.12, s32[12]{0:T(128)} %bitcast.13), custom_call_target="tpu_custom_call" | custom-call | tf_op jit(solution)/shard_map/extend_add_eliminate/pallas_call | solution.py:377
  68.3 1.8 %copy.7 = bf16[1,768,256]{2,1,0:T(8,128)(2,1)} copy(bf16[1,768,256]{2,1,0:T(8,128)(2,1)} %bitcast.8) | data formatting | bytes 786432

commit v4 on v3

--- a/solution.py
+++ b/solution.py
@@ -53,47 +53,52 @@
         pltpu.make_async_copy(front, fv, lsem.at[1]),
         pltpu.make_async_copy(winv, wv, lsem.at[2]),
     ]
-    for c in loads:
-        c.start()
+    loads[0].start()
 
     targets = []
     for s in range(6):
         child = pat[0, s]
         targets.append(jnp.where(child >= 0, fmap[jnp.maximum(child, 0)], -1))
     loads[0].wait()
+    loads[1].start()
+    loads[2].start()
 
     def c_copy(i):
         return remote(sc.at[i], cr.at[i], csend.at[i], crecv.at[i], core_peer)
 
-    for i in ORDER:
-        def masks(y, c):
-            block = y * 2 + c + 4 * i
-            return [(t == block).astype(F32) for t in targets]
-
-        away = [masks(y, 1 - core) for y in range(2)]
-        stay = [masks(y, core) for y in range(2)]
+    def totals(i, c, put):
+        masks = [[(t == y * 2 + c + 4 * i).astype(F32) for t in targets] for y in range(2)]
 
         def tile(t, carry):
             rows = pl.ds(pl.multiple_of(t * 32, 32), 32)
             vals = [cv[s, rows, :].astype(F32) for s in range(6)]
-
-            def total(ms):
-                acc = vals[0] * ms[0]
-                for v, m in zip(vals[1:], ms[1:]):
+            for y in range(2):
+                acc = vals[0] * masks[y][0]
+                for v, m in zip(vals[1:], masks[y][1:]):
                     acc = acc + v * m
-                return acc
-
-            for y in range(2):
-                sc[i, y, rows, :] = total(away[y]).astype(BF16)
-            for y in range(2):
-                own[i, y, rows, :] = total(stay[y])
+                put(y, rows, acc)
             return carry
 
         lax.fori_loop(0, 8, tile, 0)
 
-    pl.semaphore_wait(barrier, len(peers))
+    def put_away(i):
+        def put(y, rows, acc):
+            sc[i, y, rows, :] = acc.astype(BF16)
+
+        return put
+
+    def put_own(i):
+        def put(y, rows, acc):
+            own[i, y, rows, :] = acc
+
+        return put
+
     for i in ORDER:
+        totals(i, 1 - core, put_away(i))
+        if i == ORDER[0]:
+            pl.semaphore_wait(barrier, len(peers))
         c_copy(i).start()
+        totals(i, core, put_own(i))
 
     own_half = pl.ds(pl.multiple_of(half * 128, 128), 128)
     far_half = pl.ds(pl.multiple_of((1 - half) * 128, 128), 128)
@@ -104,11 +109,8 @@
     def both(i, y, rows):
         return own[i, y, rows, :] + cr[i, y, rows, :].astype(F32)
 
-    for n, i in enumerate(ORDER):
+    for i in ORDER:
         c_copy(i).wait_recv()
-        if n:
-            for m in (1, 2, 3):
-                y_copy(m, ORDER[n - 1]).wait_send()
         ys[2, i] = both(i, 1 - ylo, far_half).astype(BF16)
         y_copy(3, i).start()
         ys[1, i] = both(i, ylo, far_half).astype(BF16)
@@ -120,12 +122,36 @@
     def z_copy(j, i):
         return remote(zs.at[j, i], zr.at[j, i], zsend.at[j, i], zrecv.at[j, i], z_peer)
 
+    first = half == 0
+
+    def near_sum(j, i):
+        y_copy(1, i).wait_recv()
+        zs[j, i] = (kept[i] + yr[0, i].astype(F32)).astype(BF16)
+
+    def far_sum(j, i):
+        y_copy(2, i).wait_recv()
+        y_copy(3, i).wait_recv()
+        zs[j, i] = (yr[1, i].astype(F32) + yr[2, i].astype(F32)).astype(BF16)
+
     for i in ORDER:
-        for m in (1, 2, 3):
-            y_copy(m, i).wait_recv()
-        zs[half, i] = (kept[i] + yr[0, i].astype(F32)).astype(BF16)
-        zs[1 - half, i] = (yr[1, i].astype(F32) + yr[2, i].astype(F32)).astype(BF16)
+        @pl.when(first)
+        def _():
+            near_sum(0, i)
+
+        @pl.when(jnp.logical_not(first))
+        def _():
+            far_sum(0, i)
+
         z_copy(0, i).start()
+
+    for i in range(3):
+        @pl.when(first)
+        def _():
+            far_sum(1, i)
+
+        @pl.when(jnp.logical_not(first))
+        def _():
+            near_sum(1, i)
 
     loads[1].wait()
     f_copy = remote(fv.at[:, far_half], fx, fsend, frecv, y_peers[2])
@@ -142,7 +168,6 @@
             l_st[k, rows_of(0), :] = jnp.zeros((128, 256), BF16)
 
     f_copy.wait_recv()
-    first = half == 0
 
     def g_copy(m, i):
         ref = a_st.at[xpos, rows_of(i)]
@@ -163,8 +188,8 @@
     def tri_place(k, r, h):
         return a_st.at[k, pl.ds(pl.multiple_of(r * 256 + h * 128, 128), 128)]
 
-    def lead_place(h):
-        return a_st.at[:, pl.ds(pl.multiple_of(LEAD_ROWS + h * 128, 128), 128)]
+    def lead_place(k, h):
+        return a_st.at[k, pl.ds(pl.multiple_of(LEAD_ROWS + h * 128, 128), 128)]
 
     def t_copy(m, k):
         ref = tri_place(k, row, half)
@@ -183,18 +208,18 @@
         ref = tri_place(k, r ^ 1, h)
         return remote(ref, ref, usend.at[m, k], urecv.at[m, k], core_peer)
 
-    def q_copy(m):
-        src = a_st.at[:, rows_of(1)]
-        return remote(src, lead_place(half), qsend.at[m - 1], qrecv.at[m - 1], y_peers[m])
-
-    def q_arrival(m):
-        ref = lead_place(owner(m)[1])
-        return remote(ref, ref, qsend.at[m - 1], qrecv.at[m - 1], y_peers[m])
-
-    def v_copy(m):
-        ref = lead_place(owner(m)[1])
-        src = a_st.at[:, rows_of(1)] if m == 0 else ref
-        return remote(src, ref, vsend.at[m], vrecv.at[m], core_peer)
+    def q_copy(m, k):
+        src = a_st.at[k, rows_of(1)]
+        return remote(src, lead_place(k, half), qsend.at[m - 1, k], qrecv.at[m - 1, k], y_peers[m])
+
+    def q_arrival(m, k):
+        ref = lead_place(k, owner(m)[1])
+        return remote(ref, ref, qsend.at[m - 1, k], qrecv.at[m - 1, k], y_peers[m])
+
+    def v_copy(m, k):
+        ref = lead_place(k, owner(m)[1])
+        src = a_st.at[k, rows_of(1)] if m == 0 else ref
+        return remote(src, ref, vsend.at[m, k], vrecv.at[m, k], core_peer)
 
     def each(count, body):
         def step(k, carry):
@@ -203,59 +228,69 @@
 
         lax.fori_loop(0, count, step, 0)
 
+    def send_lead(k):
+        @pl.when(row == xpos)
+        def _():
+            for m in (3, 1, 2):
+                q_copy(m, k).start()
+            v_copy(0, k).start()
+
+    def send_tri(k):
+        @pl.when(row > k)
+        def _():
+            for m in (3, 1, 2):
+                t_copy(m, k).start()
+            u_copy(0, k).start()
+
     critical(1)
-    for m in (1, 2, 3):
+    for m in (1, 3, 2):
         g_copy(m, 1).start()
+    send_lead(xpos)
     z_copy(1, 0).start()
 
     critical(0)
 
     @pl.when(row > xpos)
     def _():
-        for m in (1, 2, 3):
+        for m in (1, 3, 2):
             g_copy(m, 0).start()
 
+    send_tri(xpos)
     z_copy(1, 1).start()
 
-    for m in (1, 2, 3):
+    for m in (1, 3, 2):
         g_arrival(m, 1).wait_recv()
+        send_lead(xpos ^ m)
+
+        @pl.when(row > (xpos ^ m))
+        def _():
+            g_arrival(m, 0).wait_recv()
+
+        send_tri(xpos ^ m)
 
     @pl.when(row == xpos)
     def _():
-        for m in (3, 1, 2):
-            q_copy(m).start()
-        v_copy(0).start()
         for k in range(4):
             a_st[k, pl.ds(pl.multiple_of(LEAD_ROWS + half * 128, 128), 128), :] = a_st[k, rows_of(1), :]
 
-    for m in (1, 2, 3):
-        @pl.when(row > (xpos ^ m))
-        def _():
-            g_arrival(m, 0).wait_recv()
-
-    def send_tri(k):
-        for m in (3, 1, 2):
-            t_copy(m, k).start()
-        u_copy(0, k).start()
-
-    each(row, send_tri)
-
     critical(2)
-    for m in (1, 2, 3):
+    for m in (1, 3, 2):
         g_copy(m, 2).start()
     z_copy(1, 2).start()
 
-    for m in (1, 3, 2):
-        @pl.when(owner(m)[0] == xpos)
-        def _():
-            q_arrival(m).wait_recv()
-            v_copy(m).start()
-    for m in (1, 3, 2):
-        def relay_tri(k):
-            t_arrival(m, k).wait_recv()
-            u_copy(m, k).start()
-
-        each(owner(m)[0], relay_tri)
+    for n in (0, 1, 3, 2):
+        k = xpos ^ n
+        for m in (1, 3, 2):
+            @pl.when(owner(m)[0] == xpos)
+            def _():
+                q_arrival(m, k).wait_recv()
+                v_copy(m, k).start()
+
+            @pl.when(owner(m)[0] > k)
+            def _():
+                t_arrival(m, k).wait_recv()
+                u_copy(m, k).start()
+
     for m in range(4):
         each(owner(m)[0] ^ 1, lambda k: u_arrival(m, k).wait_recv())
     loads[2].wait()
@@ -300,7 +335,8 @@
     for m in range(4):
         @pl.when((owner(m)[0] ^ 1) == xpos)
         def _():
-            v_copy(m).wait_recv()
+            for k in range(4):
+                v_copy(m, k).wait_recv()
 
     for k in range(PANELS):
         panel(k, 5)
@@ -330,8 +366,7 @@
         c_copy(i).wait_send()
         o_copy(i).wait_send()
         for m in (1, 2, 3):
-            if i == ORDER[-1]:
-                y_copy(m, i).wait_send()
+            y_copy(m, i).wait_send()
             if i:
                 g_copy(m, i).wait_send()
 
@@ -350,12 +385,14 @@
 
         @pl.when(owner(m)[0] == xpos)
         def _():
-            v_copy(m).wait_send()
+            for k in range(4):
+                v_copy(m, k).wait_send()
 
     @pl.when(row == xpos)
     def _():
         for m in (1, 2, 3):
-            q_copy(m).wait_send()
+            for k in range(4):
+                q_copy(m, k).wait_send()
 
     for i in range(3):
         for j in range(2):
@@ -402,11 +439,11 @@
             dma(2, 3), dma(2, 3),
             dma(3, 3), dma(3, 3),
             dma(3, 3), dma(3, 3), dma(4, 3), dma(4, 3),
-            dma(3), dma(3), dma(4), dma(4),
+            dma(3, 4), dma(3, 4), dma(4, 4), dma(4, 4),
             dma(3), dma(3),
         ],
         compiler_params=pltpu.CompilerParams(
-            collective_id=0, has_side_effects=True, vmem_limit_bytes=60 * 2**20
+            collective_id=0, has_side_effects=True, vmem_limit_bytes=107 * 2**19
         ),
         name="extend_add_eliminate",
     )(front.reshape(3, 256, 256), panel_inverse[0], contrib[0], pattern[0].T, front_map[0])

time: 70.2 us -> 65.5 us (0.933)
  the two profiles are of different devices: /device:TPU:93 before, /device:TPU:61 now
where the time goes in v4:
time: 65.5 us; the launch traced here: 65.3 us
  Pallas kernels  63.9 us (98%)
  local copies, waits for them, and re-layouts  1.43 us (2%)
    pallas_call x1, Pallas kernels, shards(): pl.pallas_call(kernel, out_shape=jax.ShapeDtypeStruct((3, 256, 256), BF16...  63.9 us
    unnamed x5, local copies, waits for them, and re-layouts  1.43 us

profile of v4, /device:TPU:61, one launch (start us, length us, event | category | flops | bytes accessed | tf_op | source)
XLA Modules:
  0.0 65.3 jit_solution(449203614224833115)
XLA Ops:
  0.0 0.0 copy-start
  0.0 0.0 copy-start.1
  0.0 0.7 %copy-done = s32[1,6,2]{1,2,0:T(2,128)S(1)} copy-done((s32[1,6,2]{1,2,0:T(2,128)S(1)}, s32[1,6,2]{1,2,0:T(2,128)}, u32[]{:S(2)}) %copy-start) | copy-done | bytes 72
  0.7 0.0 copy-done.1
  0.7 63.9 %extend_add_eliminate.1 = bf16[3,256,256]{2,1,0:T(8,128)(2,1)S(1)} custom-call(bf16[3,256,256]{2,1,0:T(8,128)(2,1)} %bitcast.13, bf16[1024,256]{1,0:T(8,128)(2,1)} %bitcast.12, bf16[6,256,256]{2,1,0:T(8,128)(2,1)} %bitcast.11, s32[2,6]{1,0:T(2,128)S(1)} %bitcast.9, s32[12]{0:T(128)S(1)} %bitcast.10), custom_call_target="tpu_custom_call" | custom-call | tf_op jit(solution)/shard_map/extend_add_eliminate/pallas_call | solution.py:414
  64.5 0.7 %copy.7 = bf16[1,768,256]{2,1,0:T(8,128)(2,1)} copy(bf16[1,768,256]{2,1,0:T(8,128)(2,1)S(1)} %bitcast.8) | data formatting | bytes 786432
Async XLA Ops:
  0.0 0.7 %copy-start = (s32[1,6,2]{1,2,0:T(2,128)S(1)}, s32[1,6,2]{1,2,0:T(2,128)}, u32[]{:S(2)}) copy-start(s32[1,6,2]{1,2,0:T(2,128)} %param.8) | copy-start | bytes 148
  0.0 0.7 %copy-start.1 = (s32[1,12]{1,0:T(1,128)S(1)}, s32[1,12]{1,0:T(1,128)}, u32[]{:S(2)}) copy-start(s32[1,12]{1,0:T(1,128)} %param.9) | copy-start | bytes 148

commit v5 on v4

--- a/solution.py
+++ b/solution.py
@@ -70,7 +70,7 @@
         masks = [[(t == y * 2 + c + 4 * i).astype(F32) for t in targets] for y in range(2)]
 
         def tile(t, carry):
-            rows = pl.ds(pl.multiple_of(t * 32, 32), 32)
+            rows = pl.ds(pl.multiple_of(t * 16, 16), 16)
             vals = [cv[s, rows, :].astype(F32) for s in range(6)]
             for y in range(2):
                 acc = vals[0] * masks[y][0]
@@ -79,7 +79,7 @@
                 put(y, rows, acc)
             return carry
 
-        lax.fori_loop(0, 8, tile, 0)
+        lax.fori_loop(0, 16, tile, 0, unroll=4)
 
     def put_away(i):
         def put(y, rows, acc):

time: 65.5 us -> 64.4 us (0.983)
  the two profiles are of different devices: /device:TPU:61 before, /device:TPU:45 now
where the time goes in v5:
time: 64.4 us; the launch traced here: 64.2 us
  Pallas kernels  62.8 us (98%)
  local copies, waits for them, and re-layouts  1.43 us (2%)
    pallas_call x1, Pallas kernels, shards(): pl.pallas_call(kernel, out_shape=jax.ShapeDtypeStruct((3, 256, 256), BF16...  62.8 us
    unnamed x5, local copies, waits for them, and re-layouts  1.43 us

profile of v5, /device:TPU:45, one launch (start us, length us, event | category | flops | bytes accessed | tf_op | source)
XLA Modules:
  0.0 64.2 jit_solution(5207761784648183884)
XLA Ops:
  0.0 0.0 copy-start
  0.0 0.0 copy-start.1
  0.0 0.7 %copy-done = s32[1,6,2]{1,2,0:T(2,128)S(1)} copy-done((s32[1,6,2]{1,2,0:T(2,128)S(1)}, s32[1,6,2]{1,2,0:T(2,128)}, u32[]{:S(2)}) %copy-start) | copy-done | bytes 72
  0.7 0.0 copy-done.1
  0.7 62.8 %extend_add_eliminate.1 = bf16[3,256,256]{2,1,0:T(8,128)(2,1)S(1)} custom-call(bf16[3,256,256]{2,1,0:T(8,128)(2,1)} %bitcast.13, bf16[1024,256]{1,0:T(8,128)(2,1)} %bitcast.12, bf16[6,256,256]{2,1,0:T(8,128)(2,1)} %bitcast.11, s32[2,6]{1,0:T(2,128)S(1)} %bitcast.9, s32[12]{0:T(128)S(1)} %bitcast.10), custom_call_target="tpu_custom_call" | custom-call | tf_op jit(solution)/shard_map/extend_add_eliminate/pallas_call | solution.py:414
  63.4 0.7 %copy.7 = bf16[1,768,256]{2,1,0:T(8,128)(2,1)} copy(bf16[1,768,256]{2,1,0:T(8,128)(2,1)S(1)} %bitcast.8) | data formatting | bytes 786432
Async XLA Ops:
  0.0 0.7 %copy-start = (s32[1,6,2]{1,2,0:T(2,128)S(1)}, s32[1,6,2]{1,2,0:T(2,128)}, u32[]{:S(2)}) copy-start(s32[1,6,2]{1,2,0:T(2,128)} %param.8) | copy-start | bytes 148
  0.0 0.7 %copy-start.1 = (s32[1,12]{1,0:T(1,128)S(1)}, s32[1,12]{1,0:T(1,128)}, u32[]{:S(2)}) copy-start(s32[1,12]{1,0:T(1,128)} %param.9) | copy-start | bytes 148

commit v6 on v5

--- a/solution.py
+++ b/solution.py
@@ -79,7 +79,7 @@
                 put(y, rows, acc)
             return carry
 
-        lax.fori_loop(0, 16, tile, 0, unroll=4)
+        lax.fori_loop(0, 16, tile, 0, unroll=8)
 
     def put_away(i):
         def put(y, rows, acc):

time: 64.4 us -> 64.8 us (level)
  no operation moved by 1% of the time
where the time goes in v6:
time: 64.8 us; the launch traced here: 64.7 us
  Pallas kernels  63.2 us (98%)
  local copies, waits for them, and re-layouts  1.43 us (2%)
    pallas_call x1, Pallas kernels, shards(): pl.pallas_call(kernel, out_shape=jax.ShapeDtypeStruct((3, 256, 256), BF16...  63.2 us
    unnamed x5, local copies, waits for them, and re-layouts  1.43 us

profile of v6, /device:TPU:45, one launch (start us, length us, event | category | flops | bytes accessed | tf_op | source)
XLA Modules:
  0.0 64.7 jit_solution(14643998759630447615)
XLA Ops:
  0.0 0.0 copy-start
  0.0 0.0 copy-start.1
  0.0 0.7 %copy-done = s32[1,6,2]{1,2,0:T(2,128)S(1)} copy-done((s32[1,6,2]{1,2,0:T(2,128)S(1)}, s32[1,6,2]{1,2,0:T(2,128)}, u32[]{:S(2)}) %copy-start) | copy-done | bytes 72
  0.7 0.0 copy-done.1
  0.7 63.2 %extend_add_eliminate.1 = bf16[3,256,256]{2,1,0:T(8,128)(2,1)S(1)} custom-call(bf16[3,256,256]{2,1,0:T(8,128)(2,1)} %bitcast.13, bf16[1024,256]{1,0:T(8,128)(2,1)} %bitcast.12, bf16[6,256,256]{2,1,0:T(8,128)(2,1)} %bitcast.11, s32[2,6]{1,0:T(2,128)S(1)} %bitcast.9, s32[12]{0:T(128)S(1)} %bitcast.10), custom_call_target="tpu_custom_call" | custom-call | tf_op jit(solution)/shard_map/extend_add_eliminate/pallas_call | solution.py:414
  63.9 0.7 %copy.7 = bf16[1,768,256]{2,1,0:T(8,128)(2,1)} copy(bf16[1,768,256]{2,1,0:T(8,128)(2,1)S(1)} %bitcast.8) | data formatting | bytes 786432
Async XLA Ops:
  0.0 0.7 %copy-start = (s32[1,6,2]{1,2,0:T(2,128)S(1)}, s32[1,6,2]{1,2,0:T(2,128)}, u32[]{:S(2)}) copy-start(s32[1,6,2]{1,2,0:T(2,128)} %param.8) | copy-start | bytes 148
  0.0 0.7 %copy-start.1 = (s32[1,12]{1,0:T(1,128)S(1)}, s32[1,12]{1,0:T(1,128)}, u32[]{:S(2)}) copy-start(s32[1,12]{1,0:T(1,128)} %param.9) | copy-start | bytes 148
